TPU v7x, 32 devices: a whole 2x2x4 slice. The times are simulated.
32 devices in a mesh: dp: 16 (over z, y, x), mlp: 2 (over core).
Axes of the slice: x: 2, y: 2, z: 4, core: 2. Of those that a mesh axis runs over, the one named last changes fastest.
Arguments:
- tokens: bfloat16 [64, 197, 768], P(('dp', 'mlp')), may hold values from -6 to 6
- cotangent: bfloat16 [64, 197, 768], P(('dp', 'mlp')), may hold values from -6 to 6
- prompts: float32 [2, 50, 768], P(None, None, 'mlp'), may hold values from -6 to 6
- first_moment: float32 [2, 50, 768], P(None, None, 'mlp'), may hold values from -0.005859375 to 0.005859375
- second_moment: float32 [2, 50, 768], P(None, None, 'mlp'), may hold values from 1.3020833e-08 to 5.2083333e-08
- norm_params: float32 [2, 4, 768], replicated, may hold values from -1.2 to 1.9, as said below
- bias_rows: float32 [2, 4, 768], replicated, may hold values from -1.5 to 1.5
- qkv_weight: bfloat16 [2, 768, 2304], replicated, may hold values from -0.21875 to 0.21875
- out_weight: bfloat16 [2, 768, 768], replicated, may hold values from -0.625 to 0.625
- up_weight: bfloat16 [2, 768, 3072], P(None, None, 'mlp'), may hold values from -0.21875 to 0.21875
- up_bias: float32 [2, 3072], P(None, 'mlp'), may hold values from -1.5 to 1.5
- down_weight: bfloat16 [2, 3072, 768], P(None, 'mlp'), may hold values from -0.109375 to 0.109375
Outputs:
- activations: bfloat16 [64, 197, 768], P(('dp', 'mlp'))
- input_grad: float32 [64, 197, 768], P(('dp', 'mlp'))
- prompt_grad: float32 [2, 50, 768], P(None, None, 'mlp')
- grad_norm: float32 [], replicated
- new_first: float32 [2, 50, 768], P(None, None, 'mlp')
- new_second: float32 [2, 50, 768], P(None, None, 'mlp')
- new_prompts: float32 [2, 50, 768], P(None, None, 'mlp')
Inputs may be any that keep to these rules, and one draw needn't show every extreme that they name: `norm_params`: gains in rows 0 and 2 of the middle dimension are positive.
All inputs are finite; a program needn't handle non-finite values.
Results may differ from a plain program's by a relative error of at most 0.025.
Values may be sent and summed in bfloat16 or wider, within the bound.
A program may use at most 128 MiB of HBM per device.

v0:
```python
import functools

import jax
import jax.numpy as jnp
from jax import lax
from jax.experimental import pallas as pl
from jax.experimental.pallas import tpu as pltpu
from jax.sharding import PartitionSpec as P

HEADS = 12
STEP = 10
MESH = pl.DeviceIdType.MESH
VMEM = pltpu.VMEM
DMA = pltpu.SemaphoreType.DMA
BF16 = jnp.bfloat16
F32 = jnp.float32

norm_eps = 1e-06
clip_limit = 1.0
beta_one = 0.9
beta_two = 0.999
learn_rate = 1.5
weight_decay = 0.05
adam_eps = 1e-08
LOG2E = 1.4426950408889634


def up_to(value, step):
    return -(-value // step) * step


def mm(left, right):
    return jnp.dot(left, right, preferred_element_type=F32)


def mm_nt(left, right):
    return lax.dot_general(left, right, (((1,), (1,)), ((), ())), preferred_element_type=F32)


def mm_tn(left, right):
    return lax.dot_general(left, right, (((0,), (0,)), ((), ())), preferred_element_type=F32)


def rows_loop(count, step, body, unroll=1):
    def one(i, carry):
        body(pl.multiple_of(i * step, step))
        return carry

    lax.fori_loop(0, count // step, one, 0, unroll=unroll)


def main_kernel(
    dims,
    tok_hbm,
    cot_hbm,
    prompts_hbm,
    norms_hbm,
    bias_hbm,
    qkv_hbm,
    out_hbm,
    up_hbm,
    ub_hbm,
    dn_hbm,
    act_ref,
    igrad_ref,
    pgrad_ref,
    tok,
    cot,
    prom,
    norms,
    bias,
    w_qkv,
    w_out,
    w_up,
    ub,
    w_dn,
    seq,
    hid,
    acc,
    wide,
    x16,
    xh1,
    r1,
    xh2,
    r2,
    q_s,
    k_s,
    v_s,
    e_s,
    ri_s,
    o_s,
    gp_s,
    local_sem,
    send_sem,
    recv_sem,
):
    B, T, D, L, PN, TK, PP, S, TQ, FH = dims
    H = HEADS
    HD = D // H
    C = 768
    me = lax.axis_index("mlp")
    other = 1 - me
    half = D // 2

    barrier = pltpu.get_barrier_semaphore()
    pl.semaphore_signal(barrier, inc=1, device_id={"mlp": other}, device_id_type=MESH)

    local = {}

    def fetch(name, src, dst):
        copy = pltpu.make_async_copy(src, dst, local_sem.at[len(local)])
        copy.start()
        local[name] = copy

    mine = pl.ds(pl.multiple_of(me * half, 128), half)
    fetch("tok", tok_hbm, tok)
    fetch("norms", norms_hbm, norms)
    fetch("bias", bias_hbm, bias)
    fetch("prom", prompts_hbm, prom.at[:, :, mine])
    fetch("qkv0", qkv_hbm.at[0], w_qkv.at[0])
    fetch("out0", out_hbm.at[0], w_out.at[0])
    fetch("ub", ub_hbm, ub.at[0])
    for l in range(L):
        if l:
            fetch(f"qkv{l}", qkv_hbm.at[l], w_qkv.at[l])
            fetch(f"out{l}", out_hbm.at[l], w_out.at[l])
        fetch(f"up{l}", up_hbm.at[l], w_up.at[l, 0])
        fetch(f"dn{l}", dn_hbm.at[l], w_dn.at[l, 0])
    fetch("cot", cot_hbm, cot)

    pl.semaphore_wait(barrier, 1)
    remote = {}

    def push(name, src, dst):
        i = len(remote)
        copy = pltpu.make_async_remote_copy(
            src_ref=src,
            dst_ref=dst,
            send_sem=send_sem.at[i],
            recv_sem=recv_sem.at[i],
            device_id={"mlp": other},
            device_id_type=MESH,
        )
        copy.start()
        remote[name] = copy

    push("prom", prompts_hbm, prom.at[:, :, mine])
    push("ub", ub_hbm, ub.at[1])
    for l in range(L):
        push(f"up{l}", up_hbm.at[l], w_up.at[l, 1])
        push(f"dn{l}", dn_hbm.at[l], w_dn.at[l, 1])

    lane = lax.broadcasted_iota(jnp.int32, (1, S), 1)
    valid = (lane < T) | ((lane >= TK) & (lane < TK + PN))
    key_bias = jnp.where(valid, 0.0, -1e30).astype(F32)
    even_q = lax.broadcasted_iota(jnp.int32, (TQ, 2 * HD), 1) < HD
    even_k = lax.broadcasted_iota(jnp.int32, (S, 2 * HD), 1) < HD
    scale = HD**-0.5

    for b in range(B):
        seq[b, TK - 8 :, :] = jnp.zeros((S - TK + 8, D), F32)
    local["tok"].wait()
    for b in range(B):
        seq[b, 0:T, :] = tok[b].astype(F32)
    local["norms"].wait()
    local["bias"].wait()
    local["prom"].wait()
    remote["prom"].wait()

    def norm_rows(x):
        mean = jnp.mean(x, axis=-1, keepdims=True)
        centre = x - mean
        spread = jnp.mean(centre * centre, axis=-1, keepdims=True)
        inv = lax.rsqrt(spread + norm_eps)
        return centre * inv, inv

    def attend_forward(l):
        def pair(i, carry):
            b = i // (H // 2)
            hp = i % (H // 2)
            sl = pl.ds(pl.multiple_of(hp * 2 * HD, 2 * HD), 2 * HD)
            qr = pl.ds(pl.multiple_of(b * TQ, 16), TQ)
            kr = pl.ds(pl.multiple_of(b * S, 16), S)
            q = q_s[l, qr, sl]
            k = k_s[l, kr, sl]
            v = v_s[l, kr, sl]
            sums = []
            for h in range(2):
                here = even_k if h == 0 else jnp.logical_not(even_k)
                s = mm_nt(q, jnp.where(here, k, jnp.zeros_like(k))) + key_bias
                top = jnp.max(s, axis=1, keepdims=True)
                e = jnp.exp2((s - top) * (LOG2E * scale)).astype(BF16)
                e_s[l, b, hp * 2 + h] = e
                sums.append(mm(e, jnp.where(here, v, jnp.ones_like(v))))
            top_part = jnp.where(even_q, sums[0], sums[1])
            total = jnp.where(even_q, sums[1], sums[0])
            inv = pltpu.roll(1.0 / total, HD, 1)
            ri_s[l, b, :, sl] = inv
            o_s[l, qr, sl] = (top_part * inv).astype(BF16)
            return carry

        lax.fori_loop(0, B * H // 2, pair, 0, unroll=3)

    def attend_backward(l):
        def pair(i, carry):
            b = i // (H // 2)
            hp = i % (H // 2)
            at = pl.multiple_of(hp * 2 * HD, 2 * HD)
            sl = pl.ds(at, 2 * HD)
            qr = pl.ds(pl.multiple_of(b * TQ, 16), TQ)
            kr = pl.ds(pl.multiple_of(b * S, 16), S)
            q = q_s[l, qr, sl]
            k = k_s[l, kr, sl]
            v = v_s[l, kr, sl]
            do = x16[qr, sl].astype(F32) * ri_s[l, b, :, sl]
            prod = do * o_s[l, qr, sl].astype(F32)
            do16 = do.astype(BF16)
            dq = None
            dks, dvs = [], []
            for h in range(2):
                here_q = even_q if h == 0 else jnp.logical_not(even_q)
                here = even_k if h == 0 else jnp.logical_not(even_k)
                delta = jnp.sum(jnp.where(here_q, prod, 0.0), axis=1, keepdims=True)
                dp = mm_nt(do16, jnp.where(here, v, jnp.zeros_like(v)))
                e = e_s[l, b, hp * 2 + h]
                ds = (e.astype(F32) * (dp - delta)).astype(BF16)
                part = mm(ds, jnp.where(here, k, jnp.zeros_like(k)))
                dq = part if dq is None else dq + part
                dks.append(mm_tn(ds, q))
                dvs.append(mm_tn(e, do16))
            qrow = pl.ds(pl.multiple_of(b * S, 16), TQ)
            wide[qrow, sl] = (dq * scale).astype(BF16)
            wide[kr, pl.ds(pl.multiple_of(D + at, 128), 2 * HD)] = (
                jnp.where(even_k, dks[0], dks[1]) * scale
            ).astype(BF16)
            wide[kr, pl.ds(pl.multiple_of(2 * D + at, 128), 2 * HD)] = jnp.where(
                even_k, dvs[0], dvs[1]
            ).astype(BF16)
            return carry

        lax.fori_loop(0, B * H // 2, pair, 0, unroll=3)

    for l in range(L):
        for b in range(B):
            seq[b, TK : TK + PN, :] = prom[l]
        gain, shift = norms[l, 0:1, :], norms[l, 1:2, :]
        for b in range(B):

            def ln_one(r, b=b):
                xh, inv = norm_rows(seq[b, pl.ds(r, 32), :])
                at = pl.ds(pl.multiple_of(b * S + r, 32), 32)
                xh1[l, at, :] = xh.astype(BF16)
                r1[l, at, :] = inv
                wide[at, 0:D] = (xh * gain + shift).astype(BF16)

            rows_loop(S, 32, ln_one, unroll=2)
        local[f"qkv{l}"].wait()
        lhs = jnp.concatenate([wide[b * S : b * S + TQ, 0:D] for b in range(B)], axis=0)
        q_s[l] = (mm(lhs, w_qkv[l, :, 0:D]) + bias[l, 0:1, :]).astype(BF16)
        k_s[l] = mm(wide[:, 0:D], w_qkv[l, :, D : 2 * D]).astype(BF16)
        v_s[l] = (mm(wide[:, 0:D], w_qkv[l, :, 2 * D : 3 * D]) + bias[l, 1:2, :]).astype(BF16)
        attend_forward(l)
        local[f"out{l}"].wait()
        branch = mm(o_s[l], w_out[l]) + bias[l, 2:3, :]
        for b in range(B):
            hid[b * TQ : (b + 1) * TQ, :] = seq[b, 0:TQ, :] + branch[b * TQ : (b + 1) * TQ]
        gain2, shift2 = norms[l, 2:3, :], norms[l, 3:4, :]

        def ln_two(r):
            at = pl.ds(r, 32)
            xh, inv = norm_rows(hid[at, :])
            xh2[l, at, :] = xh.astype(BF16)
            r2[l, at, :] = inv
            x16[at, :] = (xh * gain2 + shift2).astype(BF16)

        rows_loop(B * TQ, 32, ln_two)
        if l == 0:
            local["ub"].wait()
            remote["ub"].wait()
        for part in range(2):
            kept = local if part == 0 else remote
            kept[f"up{l}"].wait()
            kept[f"dn{l}"].wait()
            for j in range(FH // C):
                cols = slice(j * C, (j + 1) * C)
                pre = mm(x16[...], w_up[l, part, :, cols]) + ub[part, l : l + 1, cols]
                cdf = 0.5 + 0.5 * lax.erf(pre * 0.7071067811865476)
                bell = jnp.exp2(pre * pre * (-0.5 * LOG2E)) * 0.3989422804014327
                at = slice((part * (FH // C) + j) * C, (part * (FH // C) + j + 1) * C)
                gp_s[l, :, at] = (cdf + pre * bell).astype(BF16)
                add = mm((pre * cdf).astype(BF16), w_dn[l, part, cols, :])
                if part == 0 and j == 0:
                    acc[...] = add
                else:
                    acc[...] += add
        for b in range(B):
            seq[b, 0:TQ, :] = (
                hid[b * TQ : (b + 1) * TQ, :] + acc[b * TQ : (b + 1) * TQ, :] + bias[l, 3:4, :]
            )

    for b in range(B):
        act_ref[b] = seq[b, 0:T, :].astype(BF16)

    local["cot"].wait()
    for b in range(B):
        hid[b * TQ + TK - 8 : (b + 1) * TQ, :] = jnp.zeros((TQ - TK + 8, D), F32)
        hid[b * TQ : b * TQ + T, :] = cot[b].astype(F32)
        wide[b * S + TQ : (b + 1) * S, 0:D] = jnp.zeros((S - TQ, D), BF16)
    for l in reversed(range(L)):
        x16[...] = hid[...].astype(BF16)
        for part in range(2):
            for j in range(FH // C):
                cols = slice(j * C, (j + 1) * C)
                at = slice((part * (FH // C) + j) * C, (part * (FH // C) + j + 1) * C)
                ga = mm_nt(x16[...], w_dn[l, part, cols, :])
                gpre = (gp_s[l, :, at].astype(F32) * ga).astype(BF16)
                add = mm_nt(gpre, w_up[l, part, :, cols])
                if part == 0 and j == 0:
                    acc[...] = add
                else:
                    acc[...] += add
        gain2 = norms[l, 2:3, :]

        def ln_two_back(r):
            at = pl.ds(r, 32)
            xh = xh2[l, at, :].astype(F32)
            gdy = acc[at, :] * gain2
            a = jnp.mean(gdy, axis=-1, keepdims=True)
            c = jnp.mean(gdy * xh, axis=-1, keepdims=True)
            new = hid[at, :] + r2[l, at, :] * (gdy - a - xh * c)
            hid[at, :] = new
            x16[at, :] = new.astype(BF16)

        rows_loop(B * TQ, 32, ln_two_back)
        x16[...] = mm_nt(x16[...], w_out[l]).astype(BF16)
        attend_backward(l)
        gain = norms[l, 0:1, :]
        gn = mm_nt(wide[...], w_qkv[l])
        for b in range(B):
            seq[b] = gn[b * S : (b + 1) * S]

        def ln_back(dy, xh, inv):
            gdy = dy * gain
            a = jnp.mean(gdy, axis=-1, keepdims=True)
            c = jnp.mean(gdy * xh, axis=-1, keepdims=True)
            return inv * (gdy - a - xh * c)

        dprom = seq[0, TK:S, :]
        for b in range(1, B):
            dprom = dprom + seq[b, TK:S, :]
        xh_p = xh1[l, TK - 8 : S, :].astype(F32)[8:]
        pgrad_ref[l] = ln_back(dprom, xh_p, r1[l, TK:S, :])
        for b in range(B):

            def ln_one_back(r, b=b):
                dx = ln_back(
                    seq[b, pl.ds(r, 16), :],
                    xh1[l, pl.ds(pl.multiple_of(b * S + r, 16), 16), :].astype(F32),
                    r1[l, pl.ds(pl.multiple_of(b * S + r, 16), 16), :],
                )
                at = pl.ds(pl.multiple_of(b * TQ + r, 16), 16)
                hid[at, :] = hid[at, :] + dx

            rows_loop(TK // 16 * 16, 16, ln_one_back, unroll=2)
            base = TK // 16 * 16
            dx = ln_back(
                seq[b, base:TK, :],
                xh1[l, b * S + base : b * S + base + 16, :].astype(F32)[: TK - base],
                r1[l, b * S + base : b * S + TK, :],
            )
            hid[b * TQ + base : b * TQ + TK, :] = hid[b * TQ + base : b * TQ + TK, :] + dx
    for b in range(B):
        igrad_ref[b] = hid[b * TQ : b * TQ + T, :]


def run_main(tokens, cotangent, prompts, norm_params, bias_rows, qkv, out, up, ub, dn):
    B, T, D = tokens.shape
    L, PN, _ = prompts.shape
    FH = dn.shape[1]
    TK, PP = up_to(T, 8), up_to(PN, 8)
    S = up_to(TK + PP, 128)
    TQ = up_to(T, 16)
    dims = (B, T, D, L, PN, TK, PP, S, TQ, FH)
    H = HEADS
    n_local, n_remote = 8 + 4 * L, 2 + 2 * L
    scratch = [
        VMEM((B, T, D), BF16),
        VMEM((B, T, D), BF16),
        VMEM((L, PN, D), F32),
        VMEM((L, 4, D), F32),
        VMEM((L, 4, D), F32),
        VMEM((L, D, 3 * D), BF16),
        VMEM((L, D, D), BF16),
        VMEM((L, 2, D, FH), BF16),
        VMEM((2, L, FH), F32),
        VMEM((L, 2, FH, D), BF16),
        VMEM((B, S, D), F32),
        VMEM((B * TQ, D), F32),
        VMEM((B * TQ, D), F32),
        VMEM((B * S, 3 * D), BF16),
        VMEM((B * TQ, D), BF16),
        VMEM((L, B * S, D), BF16),
        VMEM((L, B * S, 1), F32),
        VMEM((L, B * TQ, D), BF16),
        VMEM((L, B * TQ, 1), F32),
        VMEM((L, B * TQ, D), BF16),
        VMEM((L, B * S, D), BF16),
        VMEM((L, B * S, D), BF16),
        VMEM((L, B, H, TQ, S), BF16),
        VMEM((L, B, TQ, D), F32),
        VMEM((L, B * TQ, D), BF16),
        VMEM((L, B * TQ, 2 * FH), BF16),
        DMA((n_local,)),
        DMA((n_remote,)),
        DMA((n_remote,)),
    ]
    any_spec = pl.BlockSpec(memory_space=pl.ANY)
    vmem_spec = pl.BlockSpec(memory_space=VMEM)
    return pl.pallas_call(
        functools.partial(main_kernel, dims),
        out_shape=(
            jax.ShapeDtypeStruct((B, T, D), BF16),
            jax.ShapeDtypeStruct((B, T, D), F32),
            jax.ShapeDtypeStruct((L, S - TK, D), F32),
        ),
        in_specs=[any_spec] * 10,
        out_specs=(vmem_spec,) * 3,
        scratch_shapes=scratch,
        compiler_params=pltpu.CompilerParams(
            collective_id=0, has_side_effects=True, vmem_limit_bytes=64 * 2**20
        ),
    )(tokens, cotangent, prompts, norm_params, bias_rows, qkv, out, up, ub, dn)


def tail_kernel(
    ndp, pn, pg_ref, prompt_ref, first_ref, second_ref,
    grad_ref, norm_ref, new_first_ref, new_second_ref, new_prompt_ref,
    sent, got, got0, sq, send_sem, recv_sem, half_sem, sq_sem,
):
    me = lax.axis_index("dp")
    core = lax.axis_index("mlp")
    other = 1 - core
    L, rows, D = pg_ref.shape
    half = D // 2
    steps = []
    stride = 1
    while stride < ndp:
        low = lax.rem(me, stride)
        bit = lax.rem(me // stride, 2)
        high = me // (2 * stride)
        steps.append(high * 2 * stride + (1 - bit) * stride + low)
        stride *= 2
    barrier = pltpu.get_barrier_semaphore()
    pl.semaphore_signal(barrier, inc=1, device_id={"mlp": other}, device_id_type=MESH)
    for peer in steps:
        pl.semaphore_signal(barrier, inc=1, device_id={"dp": peer}, device_id_type=MESH)
    pl.semaphore_wait(barrier, 1 + len(steps))

    def swap(src, dst, sems, device):
        copy = pltpu.make_async_remote_copy(
            src_ref=src, dst_ref=dst, send_sem=sems[0], recv_sem=sems[1],
            device_id=device, device_id_type=MESH,
        )
        copy.start()
        copy.wait()

    theirs = pl.ds(pl.multiple_of(other * half, 128), half)
    ours = pl.ds(pl.multiple_of(core * half, 128), half)
    swap(pg_ref.at[:, :, theirs], got0, (half_sem.at[0], half_sem.at[1]), {"mlp": other})
    total = pg_ref[:, :, ours] + got0[...]
    for i, peer in enumerate(steps):
        sent[i] = total
        swap(sent.at[i], got.at[i], (send_sem.at[i], recv_sem.at[i]), {"dp": peer})
        total = sent[i] + got[i]
    total = total[:, :pn]
    grad_ref[...] = total
    sq[0] = jnp.broadcast_to(jnp.sum(total * total).reshape(1, 1), (8, 128))
    swap(sq.at[0], sq.at[1], (sq_sem.at[0], sq_sem.at[1]), {"mlp": other})
    squares = sq[0, 0:1, 0:1] + sq[1, 0:1, 0:1]
    grad_norm = jnp.sqrt(squares)
    norm_ref[...] = grad_norm
    factor = jnp.minimum(1.0, clip_limit / (grad_norm + 1e-06))
    clipped = total * factor
    new_first = beta_one * first_ref[...] + (1.0 - beta_one) * clipped
    new_second = beta_two * second_ref[...] + (1.0 - beta_two) * clipped * clipped
    fix_first = 1.0 - beta_one**STEP
    fix_second = 1.0 - beta_two**STEP
    new_first_ref[...] = new_first
    new_second_ref[...] = new_second
    new_prompt_ref[...] = prompt_ref[...] - learn_rate * (
        new_first / fix_first / (jnp.sqrt(new_second / fix_second) + adam_eps)
        + weight_decay * prompt_ref[...]
    )


def run_tail(ndp, pgrad, prompts, first, second):
    L, rows, D = pgrad.shape
    n = max(1, (ndp - 1).bit_length())
    spec = pl.BlockSpec(memory_space=VMEM)
    small = jax.ShapeDtypeStruct(prompts.shape, F32)
    return pl.pallas_call(
        functools.partial(tail_kernel, ndp, prompts.shape[1]),
        out_shape=(small, jax.ShapeDtypeStruct((1, 1), F32), small, small, small),
        in_specs=[spec] * 4,
        out_specs=(spec,) * 5,
        scratch_shapes=[
            VMEM((n, L, rows, D // 2), F32),
            VMEM((n, L, rows, D // 2), F32),
            VMEM((L, rows, D // 2), F32),
            VMEM((2, 8, 128), F32),
            DMA((n,)),
            DMA((n,)),
            DMA((2,)),
            DMA((2,)),
        ],
        compiler_params=pltpu.CompilerParams(collective_id=1, has_side_effects=True),
    )(pgrad, prompts, first, second)


def local(
    ndp, tokens, cotangent, prompts, first_moment, second_moment, norm_params, bias_rows,
    qkv_weight, out_weight, up_weight, up_bias, down_weight,
):
    act, igrad, pgrad = run_main(
        tokens, cotangent, prompts, norm_params, bias_rows,
        qkv_weight, out_weight, up_weight, up_bias, down_weight,
    )
    grad, norm, new_first, new_second, new_prompts = run_tail(
        ndp, pgrad, prompts, first_moment, second_moment
    )
    return act, igrad, grad, norm.reshape(()), new_first, new_second, new_prompts


def solution(mesh):
    ndp = mesh.shape["dp"]
    return jax.shard_map(
        functools.partial(local, ndp),
        mesh=mesh,
        in_specs=(
            P(("dp", "mlp"), None, None),
            P(("dp", "mlp"), None, None),
            P(None, None, "mlp"),
            P(None, None, "mlp"),
            P(None, None, "mlp"),
            P(),
            P(),
            P(),
            P(),
            P(None, None, "mlp"),
            P(None, "mlp"),
            P(None, "mlp", None),
        ),
        out_specs=(
            P(("dp", "mlp"), None, None),
            P(("dp", "mlp"), None, None),
            P(None, None, "mlp"),
            P(),
            P(None, None, "mlp"),
            P(None, None, "mlp"),
            P(None, None, "mlp"),
        ),
        check_vma=False,
    )
```

profile of v0, /device:TPU:0, one launch (start us, length us, event | category | flops | bytes accessed | tf_op | source)
XLA Modules:
  0.0 129.8 jit_solution(16305332001520737609)
XLA Ops:
  0.6 2.0 %copy.19.tok_hbm = bf16[2,197,768]{2,1,0:T(8,128)(2,1)} copy(bf16[2,197,768]{2,0,1:T(2,128)(2,1)} %param.12) | data formatting | bytes 1210368 | tf_op args[0]
  2.6 2.0 %copy.20.cot_hbm = bf16[2,197,768]{2,1,0:T(8,128)(2,1)} copy(bf16[2,197,768]{2,0,1:T(2,128)(2,1)} %param.13) | data formatting | bytes 1210368 | tf_op args[1]
  4.6 1.6 %copy.21.prompts_hbm.prompt_ref = f32[2,50,384]{2,1,0:T(8,128)} copy(f32[2,50,384]{2,0,1:T(2,128)} %param.14) | data formatting | bytes 307200 | tf_op args[2]
  6.2 73.6 %shard_map.171 = (bf16[2,197,768]{2,1,0:T(8,128)(2,1)}, f32[2,197,768]{2,1,0:T(8,128)}, f32[2,56,768]{2,1,0:T(8,128)}) custom-call(bf16[2,197,768]{2,1,0:T(8,128)(2,1)} %copy.19.tok_hbm, bf16[2,197,768]{2,1,0:T(8,128)(2,1)} %copy.20.cot_hbm, f32[2,50,384]{2,1,0:T(8,128)} %copy.21.prompts_hbm.prompt_ref, f32[2,4,768]{2,1,0:T(4,128)} %norms_hbm.1, ...), custom_call_target="tpu_custom_call" | custom-call | tf_op jit(solution)/shard_map/pallas_call | solution.py:419
  79.7 2.4 %copy.25 = bf16[2,197,768]{2,0,1:T(2,128)(2,1)} copy(bf16[2,197,768]{2,1,0:T(8,128)(2,1)} %get-tuple-element.23) | data formatting | bytes 1210368
  82.1 2.9 %copy.26 = f32[2,197,768]{2,0,1:T(2,128)} copy(f32[2,197,768]{2,1,0:T(8,128)} %get-tuple-element.24) | data formatting | bytes 2420736
  85.0 1.6 %copy.23.first_ref = f32[2,50,384]{2,1,0:T(8,128)} copy(f32[2,50,384]{2,0,1:T(2,128)} %param.15) | data formatting | bytes 307200 | tf_op args[3]
  86.6 1.6 %copy.24.second_ref = f32[2,50,384]{2,1,0:T(8,128)} copy(f32[2,50,384]{2,0,1:T(2,128)} %param.16) | data formatting | bytes 307200 | tf_op args[4]
  88.2 33.3 %shard_map.172 = (f32[2,50,384]{2,1,0:T(8,128)}, f32[1,1]{1,0:T(1,128)}, f32[2,50,384]{2,1,0:T(8,128)}, f32[2,50,384]{2,1,0:T(8,128)}, f32[2,50,384]{2,1,0:T(8,128)}) custom-call(f32[2,56,768]{2,1,0:T(8,128)} %get-tuple-element.17.pg_ref, f32[2,50,384]{2,1,0:T(8,128)} %copy.21.prompts_hbm.prompt_ref, f32[2,50,384]{2,1,0:T(8,128)} %copy.23.first_ref, ...), custom_call_target="tpu_custom_call" | custom-call | tf_op jit(solution)/shard_map/pallas_call | solution.py:501
  121.5 1.7 %copy.27 = f32[2,50,384]{2,0,1:T(2,128)} copy(f32[2,50,384]{2,1,0:T(8,128)} %get-tuple-element.25) | data formatting | bytes 307200
  123.1 1.7 %copy.28 = f32[2,50,384]{2,0,1:T(2,128)} copy(f32[2,50,384]{2,1,0:T(8,128)} %get-tuple-element.27) | data formatting | bytes 307200
  124.8 1.7 %copy.29 = f32[2,50,384]{2,0,1:T(2,128)} copy(f32[2,50,384]{2,1,0:T(8,128)} %get-tuple-element.28) | data formatting | bytes 307200
  126.5 1.7 %copy.30 = f32[2,50,384]{2,0,1:T(2,128)} copy(f32[2,50,384]{2,1,0:T(8,128)} %get-tuple-element.29) | data formatting | bytes 307200
where the time goes:
time: 130 us
  Pallas kernels  107 us (82%)
  local copies, waits for them, and re-layouts  20.6 us (16%)
  between operations  2.35 us (2%)
    pallas_call x1, Pallas kernels, run_main(): pl.pallas_call(functools.partial(main_kernel, dims), out_shape=(jax.Shape...  73.6 us
    pallas_call x1, Pallas kernels, run_tail(): pl.pallas_call(functools.partial(tail_kernel, ndp, prompts.shape[1]), out...  33.3 us
    unnamed x11, local copies, waits for them, and re-layouts  20.6 us

commit v1 on v0

v1 whole, which is shorter than its diff:
```python
import functools

import jax
import jax.numpy as jnp
from jax import lax
from jax.experimental import pallas as pl
from jax.experimental.pallas import tpu as pltpu
from jax.sharding import PartitionSpec as P

HEADS = 12
STEP = 10
MESH = pl.DeviceIdType.MESH
VMEM = pltpu.VMEM
DMA = pltpu.SemaphoreType.DMA
BF16 = jnp.bfloat16
F32 = jnp.float32

norm_eps = 1e-06
clip_limit = 1.0
beta_one = 0.9
beta_two = 0.999
learn_rate = 1.5
weight_decay = 0.05
adam_eps = 1e-08
LOG2E = 1.4426950408889634


def up_to(value, step):
    return -(-value // step) * step


def mm(left, right):
    return jnp.dot(left, right, preferred_element_type=F32)


def mm_nt(left, right):
    return lax.dot_general(left, right, (((1,), (1,)), ((), ())), preferred_element_type=F32)


def mm_tn(left, right):
    return lax.dot_general(left, right, (((0,), (0,)), ((), ())), preferred_element_type=F32)


def rows_loop(count, step, body, unroll=1):
    def one(i, carry):
        body(pl.multiple_of(i * step, step))
        return carry

    lax.fori_loop(0, count // step, one, 0, unroll=unroll)


def main_kernel(
    dims,
    tok_hbm,
    cot_hbm,
    prompts_hbm,
    first_hbm,
    second_hbm,
    norms_hbm,
    bias_hbm,
    qkv_hbm,
    out_hbm,
    up_hbm,
    ub_hbm,
    dn_hbm,
    act_hbm,
    igrad_hbm,
    pgrad_hbm,
    norm_hbm,
    new_first_hbm,
    new_second_hbm,
    new_prompt_hbm,
    tok_nat,
    cot_nat,
    stage_nat,
    prom_nat,
    adam_nat,
    norms,
    bias,
    w_qkv,
    w_out,
    w_up,
    ub,
    w_dn,
    seq,
    hid,
    acc,
    wide,
    x16,
    xh1,
    r1,
    xh2,
    r2,
    q_s,
    k_s,
    v_s,
    e_s,
    ri_s,
    o_s,
    gp_s,
    part_f,
    part_h,
    got_a,
    sum_b,
    sum_h,
    slot_b,
    slot_c,
    fin,
    sq,
    norm_s,
    local_sem,
    out_sem,
    send_sem,
    recv_sem,
    sem_a,
    send_b,
    recv_b,
    send_c,
    recv_c,
    send_d,
    recv_d,
    sem_sq,
):
    B, T, D, L, PN, TK, S, TQ, FH, G, R = dims
    H = HEADS
    HD = D // H
    C = 768
    NJ = D // 128
    HJ = NJ // 2
    PB = 16
    core = lax.axis_index("mlp")
    other = 1 - core
    me = lax.axis_index("dp")
    g, r = lax.rem(me, G), me // G
    half = D // 2

    def member(k):
        return lax.rem(g + k, G)

    def rank(k):
        return lax.rem(r + k, R)

    barrier = pltpu.get_barrier_semaphore()
    pl.semaphore_signal(barrier, inc=1, device_id={"mlp": other}, device_id_type=MESH)
    for k in range(1, G):
        pl.semaphore_signal(
            barrier, inc=1, device_id={"dp": r * G + member(k)}, device_id_type=MESH
        )

    def greet(k, carry):
        pl.semaphore_signal(
            barrier, inc=1, device_id={"dp": rank(k) * G + g}, device_id_type=MESH
        )
        return carry

    lax.fori_loop(1, R, greet, 0)

    local = {}

    def fetch(name, src, dst):
        copy = pltpu.make_async_copy(src, dst, local_sem.at[len(local)])
        copy.start()
        local[name] = copy

    def fetch_native(name, src, dst, base, count):
        for j in range(count):
            fetch(f"{name}{j}", src.at[:, :, 128 * j : 128 * (j + 1)], dst.at[base + j])

    fetch_native("tok", tok_hbm, tok_nat, 0, NJ)
    fetch_native("prom", prompts_hbm, prom_nat, core * HJ, HJ)
    fetch("norms", norms_hbm, norms)
    fetch("bias", bias_hbm, bias)
    fetch("qkv0", qkv_hbm.at[0], w_qkv.at[0])

    remote = {}

    def push(name, src, dst):
        i = len(remote)
        copy = pltpu.make_async_remote_copy(
            src_ref=src,
            dst_ref=dst,
            send_sem=send_sem.at[i],
            recv_sem=recv_sem.at[i],
            device_id={"mlp": other},
            device_id_type=MESH,
        )
        copy.start()
        remote[name] = copy

    pl.semaphore_wait(barrier, G + R - 1)
    for j in range(HJ):
        push(
            f"prom{j}",
            prompts_hbm.at[:, :, 128 * j : 128 * (j + 1)],
            prom_nat.at[core * HJ + j],
        )

    tok_v = tok_nat.reshape(NJ, T * B, 128)
    cot_v = cot_nat.reshape(NJ, T * B, 128)
    stage_v = stage_nat.reshape(NJ, T * B, 128)
    prom_v = prom_nat.reshape(NJ, PN * L, 128)

    lane = lax.broadcasted_iota(jnp.int32, (1, S), 1)
    valid = (lane < T) | ((lane >= TK) & (lane < TK + PN))
    key_bias = jnp.where(valid, 0.0, -1e30).astype(F32)
    even_q = lax.broadcasted_iota(jnp.int32, (TQ, 2 * HD), 1) < HD
    even_k = lax.broadcasted_iota(jnp.int32, (S, 2 * HD), 1) < HD
    SH = S // 2
    even_h = lax.broadcasted_iota(jnp.int32, (SH, 2 * HD), 1) < HD
    low_lane = lax.broadcasted_iota(jnp.int32, (TQ, S), 1) < SH
    scale = HD**-0.5

    def spread(src_v, store):
        for j in range(NJ):
            stage_v[j] = src_v[j].astype(F32)
        for b in range(B):
            for j in range(NJ):
                store(b, slice(128 * j, 128 * (j + 1)), stage_v[j, pl.ds(b, T, stride=B), :])

    for b in range(B):
        seq[b, TK - 8 :, :] = jnp.zeros((S - TK + 8, D), F32)
    for j in range(NJ):
        local[f"tok{j}"].wait()

    def store_tok(b, cols, rows):
        seq[b, 0:T, cols] = rows

    spread(tok_v, store_tok)
    local["norms"].wait()
    local["bias"].wait()
    for j in range(HJ):
        local[f"prom{j}"].wait()
        remote[f"prom{j}"].wait()

    def norm_rows(x):
        mean = jnp.mean(x, axis=-1, keepdims=True)
        centre = x - mean
        spread_ = jnp.mean(centre * centre, axis=-1, keepdims=True)
        inv = lax.rsqrt(spread_ + norm_eps)
        return centre * inv, inv

    def attend_forward(l):
        def pair(i, carry):
            b = i // (H // 2)
            hp = i % (H // 2)
            sl = pl.ds(pl.multiple_of(hp * 2 * HD, 2 * HD), 2 * HD)
            qr = pl.ds(pl.multiple_of(b * TQ, 16), TQ)
            kr = pl.ds(pl.multiple_of(b * S, 16), S)
            q = q_s[l, qr, sl]
            k = k_s[l, kr, sl]
            v = v_s[l, kr, sl]
            sums = []
            for h in range(2):
                here = even_k if h == 0 else jnp.logical_not(even_k)
                s = mm_nt(q, jnp.where(here, k, jnp.zeros_like(k))) + key_bias
                top = jnp.max(s, axis=1, keepdims=True)
                e = jnp.exp2((s - top) * (LOG2E * scale)).astype(BF16)
                e_s[l, b, hp * 2 + h] = e
                sums.append(mm(e, jnp.where(here, v, jnp.ones_like(v))))
            top_part = jnp.where(even_q, sums[0], sums[1])
            total = jnp.where(even_q, sums[1], sums[0])
            inv = pltpu.roll(1.0 / total, HD, 1)
            ri_s[l, b, :, sl] = inv
            o_s[l, qr, sl] = (top_part * inv).astype(BF16)
            return carry

        lax.fori_loop(0, B * H // 2, pair, 0, unroll=3)

    def back_half(l, b, hp, part, first):
        at = pl.multiple_of(hp * 2 * HD, 2 * HD)
        sl = pl.ds(at, 2 * HD)
        qr = pl.ds(pl.multiple_of(b * TQ, 16), TQ)
        kr = pl.ds(pl.multiple_of(b * S + part * SH, 16), SH)
        q = q_s[l, qr, sl]
        v = v_s[l, kr, sl]
        if first:
            do = x16[qr, sl].astype(F32) * ri_s[l, b, :, sl]
            prod = do * o_s[l, qr, sl].astype(F32)
            d0 = jnp.sum(jnp.where(even_q, prod, 0.0), axis=1, keepdims=True)
            d1 = jnp.sum(jnp.where(even_q, 0.0, prod), axis=1, keepdims=True)
            do16 = do.astype(BF16)
            x16[qr, sl] = do16
            ri_s[l, b, :, sl] = jnp.where(even_q, d0, d1)
        else:
            do16 = x16[qr, sl]
            both = ri_s[l, b, :, sl]
            d0, d1 = both[:, 0:1], both[:, HD : HD + 1]
        zero = jnp.zeros_like(v)
        stacked = jnp.concatenate([jnp.where(even_h, v, zero), jnp.where(even_h, zero, v)], axis=0)
        dp = mm_nt(do16, stacked)
        keys = slice(part * SH, (part + 1) * SH)
        e = jnp.concatenate([e_s[l, b, hp * 2, :, keys], e_s[l, b, hp * 2 + 1, :, keys]], axis=1)
        ds = (e.astype(F32) * (dp - jnp.where(low_lane, d0, d1))).astype(BF16)
        dk = mm_tn(ds, q)
        dv = mm_tn(e, do16)
        wide[kr, pl.ds(pl.multiple_of(D + at, 128), 2 * HD)] = (
            jnp.where(even_h, dk[:SH], dk[SH:]) * scale
        ).astype(BF16)
        wide[kr, pl.ds(pl.multiple_of(2 * D + at, 128), 2 * HD)] = jnp.where(
            even_h, dv[:SH], dv[SH:]
        ).astype(BF16)
        return ds

    def back_queries(l, b, hp, low, high):
        at = pl.multiple_of(hp * 2 * HD, 2 * HD)
        sl = pl.ds(at, 2 * HD)
        kr = pl.ds(pl.multiple_of(b * S, 16), S)
        k = k_s[l, kr, sl]
        zero = jnp.zeros_like(k)
        dq = mm(jnp.concatenate([low[:, :SH], high[0]], axis=1), jnp.where(even_k, k, zero))
        dq += mm(jnp.concatenate([low[:, SH:], high[1]], axis=1), jnp.where(even_k, zero, k))
        wide[pl.ds(pl.multiple_of(b * S, 16), TQ), sl] = (dq * scale).astype(BF16)

    def pairs_loop(body, lo, hi):
        def one(i, carry):
            body(i // (H // 2), i % (H // 2))
            return carry

        lax.fori_loop(lo, hi, one, 0, unroll=3)

    pairs = B * H // 2

    def device_of(member_, rank_):
        return {"dp": rank_ * G + member_}

    def copy_a(l):
        return pltpu.make_async_remote_copy(
            src_ref=part_h.at[l, other],
            dst_ref=got_a.at[l],
            send_sem=sem_a.at[l, 0],
            recv_sem=sem_a.at[l, 1],
            device_id={"mlp": other},
            device_id_type=MESH,
        )

    def copy_b(l, k):
        peer = member(k)
        return pltpu.make_async_remote_copy(
            src_ref=sum_h.at[l, peer],
            dst_ref=slot_b.at[l, g],
            send_sem=send_b.at[l, peer],
            recv_sem=recv_b.at[l, g],
            device_id=device_of(peer, r),
            device_id_type=MESH,
        )

    def copy_c(l, k):
        peer = rank(k)
        return pltpu.make_async_remote_copy(
            src_ref=slot_c.at[l, r],
            dst_ref=slot_c.at[l, r],
            send_sem=send_c.at[l, peer],
            recv_sem=recv_c.at[l, r],
            device_id=device_of(g, peer),
            device_id_type=MESH,
        )

    def copy_d(l, k):
        peer = member(k)
        return pltpu.make_async_remote_copy(
            src_ref=fin.at[l, g],
            dst_ref=fin.at[l, g],
            send_sem=send_d.at[l, peer],
            recv_sem=recv_d.at[l, g],
            device_id=device_of(peer, r),
            device_id_type=MESH,
        )

    def await_from(l, slots, sems, index):
        pltpu.make_async_remote_copy(
            src_ref=slots.at[l, index],
            dst_ref=slots.at[l, index],
            send_sem=sems.at[l, index],
            recv_sem=sems.at[l, index],
            device_id={"mlp": other},
            device_id_type=MESH,
        ).wait_recv()

    def reduce_start(l, grad):
        rows = jnp.concatenate([grad, jnp.zeros((G * PB - grad.shape[0], D), F32)], axis=0)
        for j in range(NJ):
            for k in range(G):
                block = rows[k * PB : (k + 1) * PB, 128 * j : 128 * (j + 1)]
                part_f[l, j // HJ, k, j % HJ] = block
                part_h[l, j // HJ, k, j % HJ] = block.astype(BF16)
        copy_a(l).start()

    def reduce_pair(l):
        copy_a(l).wait()
        total = part_f[l, core] + got_a[l].astype(F32)
        sum_b[l] = total
        sum_h[l] = total.astype(BF16)
        for k in range(1, G):
            copy_b(l, k).start()

    def reduce_group(l):
        total = sum_b[l, g]
        for k in range(1, G):
            await_from(l, slot_b, recv_b, member(k))
            total = total + slot_b[l, member(k)].astype(F32)
        slot_c[l, r] = total.astype(BF16)

        def go(k, carry):
            copy_c(l, k).start()
            return carry

        lax.fori_loop(1, R, go, 0)
        for k in range(1, G):
            copy_b(l, k).wait_send()

    def reduce_ranks(l):
        def come(k, carry):
            await_from(l, slot_c, recv_c, rank(k))
            return carry

        lax.fori_loop(1, R, come, 0)

        def add(k, total):
            return total + slot_c[l, k].astype(F32)

        total = lax.fori_loop(0, R, add, jnp.zeros((HJ, PB, 128), F32))
        fin[l, g] = total.astype(BF16)
        for k in range(1, G):
            copy_d(l, k).start()

        def sent(k, carry):
            copy_c(l, k).wait_send()
            return carry

        lax.fori_loop(1, R, sent, 0)

    def reduce_end(l):
        for k in range(1, G):
            await_from(l, fin, recv_d, member(k))
        for k in range(1, G):
            copy_d(l, k).wait_send()

    for l in range(L):
        for b in range(B):
            for j in range(NJ):
                seq[b, TK : TK + PN, 128 * j : 128 * (j + 1)] = prom_v[
                    j, pl.ds(l, PN, stride=L), :
                ]
        gain, shift = norms[l, 0:1, :], norms[l, 1:2, :]
        for b in range(B):

            def ln_one(row, b=b):
                xh, inv = norm_rows(seq[b, pl.ds(row, 32), :])
                at = pl.ds(pl.multiple_of(b * S + row, 32), 32)
                xh1[l, at, :] = xh.astype(BF16)
                r1[l, at, :] = inv
                wide[at, 0:D] = (xh * gain + shift).astype(BF16)

            rows_loop(S, 32, ln_one, unroll=2)
        local[f"qkv{l}"].wait()
        if l == 0:
            fetch("out0", out_hbm.at[0], w_out.at[0])
            fetch("ub", ub_hbm, ub.at[0])
            push("ub", ub_hbm, ub.at[1])
            for i in range(L):
                push(f"up{i}", up_hbm.at[i], w_up.at[i, 1])
                push(f"dn{i}", dn_hbm.at[i], w_dn.at[i, 1])
            for i in range(L):
                if i:
                    fetch(f"qkv{i}", qkv_hbm.at[i], w_qkv.at[i])
                    fetch(f"out{i}", out_hbm.at[i], w_out.at[i])
                fetch(f"up{i}", up_hbm.at[i], w_up.at[i, 0])
                fetch(f"dn{i}", dn_hbm.at[i], w_dn.at[i, 0])
            fetch_native("cot", cot_hbm, cot_nat, 0, NJ)
            for j in range(HJ):
                cols = slice(128 * j, 128 * (j + 1))
                fetch(f"first{j}", first_hbm.at[:, :, cols], adam_nat.at[0, j, 0:PN])
                fetch(f"second{j}", second_hbm.at[:, :, cols], adam_nat.at[1, j, 0:PN])
        lhs = jnp.concatenate([wide[b * S : b * S + TQ, 0:D] for b in range(B)], axis=0)
        q_s[l] = (mm(lhs, w_qkv[l, :, 0:D]) + bias[l, 0:1, :]).astype(BF16)
        k_s[l] = mm(wide[:, 0:D], w_qkv[l, :, D : 2 * D]).astype(BF16)
        v_s[l] = (mm(wide[:, 0:D], w_qkv[l, :, 2 * D : 3 * D]) + bias[l, 1:2, :]).astype(BF16)
        attend_forward(l)
        local[f"out{l}"].wait()
        branch = mm(o_s[l], w_out[l]) + bias[l, 2:3, :]
        for b in range(B):
            hid[b * TQ : (b + 1) * TQ, :] = seq[b, 0:TQ, :] + branch[b * TQ : (b + 1) * TQ]
        gain2, shift2 = norms[l, 2:3, :], norms[l, 3:4, :]

        def ln_two(row):
            at = pl.ds(row, 32)
            xh, inv = norm_rows(hid[at, :])
            xh2[l, at, :] = xh.astype(BF16)
            r2[l, at, :] = inv
            x16[at, :] = (xh * gain2 + shift2).astype(BF16)

        rows_loop(B * TQ, 32, ln_two)
        if l == 0:
            local["ub"].wait()
            remote["ub"].wait()
        for part in range(2):
            kept = local if part == 0 else remote
            kept[f"up{l}"].wait()
            kept[f"dn{l}"].wait()
            for j in range(FH // C):
                cols = slice(j * C, (j + 1) * C)
                pre = mm(x16[...], w_up[l, part, :, cols]) + ub[part, l : l + 1, cols]
                cdf = 0.5 + 0.5 * lax.erf(pre * 0.7071067811865476)
                bell = jnp.exp2(pre * pre * (-0.5 * LOG2E)) * 0.3989422804014327
                at = slice((part * (FH // C) + j) * C, (part * (FH // C) + j + 1) * C)
                gp_s[l, :, at] = (cdf + pre * bell).astype(BF16)
                add = mm((pre * cdf).astype(BF16), w_dn[l, part, cols, :])
                if part == 0 and j == 0:
                    acc[...] = add
                else:
                    acc[...] += add
        for b in range(B):
            seq[b, 0:TQ, :] = (
                hid[b * TQ : (b + 1) * TQ, :] + acc[b * TQ : (b + 1) * TQ, :] + bias[l, 3:4, :]
            )

    for b in range(B):
        for j in range(NJ):
            stage_v[j, pl.ds(b, T, stride=B), :] = seq[b, 0:T, 128 * j : 128 * (j + 1)]
    leaving = []

    def leave(src, dst):
        copy = pltpu.make_async_copy(src, dst, out_sem.at[len(leaving)])
        copy.start()
        leaving.append(copy)

    for j in range(NJ):
        tok_v[j] = stage_v[j].astype(BF16)
        leave(tok_nat.at[j], act_hbm.at[:, :, 128 * j : 128 * (j + 1)])

    for j in range(NJ):
        local[f"cot{j}"].wait()
    for b in range(B):
        hid[b * TQ + TK - 8 : (b + 1) * TQ, :] = jnp.zeros((TQ - TK + 8, D), F32)
        wide[b * S + TQ : (b + 1) * S, 0:D] = jnp.zeros((S - TQ, D), BF16)

    def store_cot(b, cols, rows):
        hid[b * TQ : b * TQ + T, cols] = rows

    spread(cot_v, store_cot)

    for l in reversed(range(L)):
        last = l == 0
        above = l + 1
        x16[...] = hid[...].astype(BF16)
        for part in range(2):
            for j in range(FH // C):
                cols = slice(j * C, (j + 1) * C)
                at = slice((part * (FH // C) + j) * C, (part * (FH // C) + j + 1) * C)
                ga = mm_nt(x16[...], w_dn[l, part, cols, :])
                gpre = (gp_s[l, :, at].astype(F32) * ga).astype(BF16)
                add = mm_nt(gpre, w_up[l, part, :, cols])
                if part == 0 and j == 0:
                    acc[...] = add
                else:
                    acc[...] += add
            if above < L:
                (reduce_pair if part == 0 else reduce_group)(above)
        gain2 = norms[l, 2:3, :]

        def ln_two_back(row):
            at = pl.ds(row, 32)
            xh = xh2[l, at, :].astype(F32)
            gdy = acc[at, :] * gain2
            a = jnp.mean(gdy, axis=-1, keepdims=True)
            c = jnp.mean(gdy * xh, axis=-1, keepdims=True)
            new = hid[at, :] + r2[l, at, :] * (gdy - a - xh * c)
            hid[at, :] = new
            x16[at, :] = new.astype(BF16)

        rows_loop(B * TQ, 32, ln_two_back)
        x16[...] = mm_nt(x16[...], w_out[l]).astype(BF16)
        gain = norms[l, 0:1, :]

        def ln_back(dy, xh, inv):
            gdy = dy * gain
            a = jnp.mean(gdy, axis=-1, keepdims=True)
            c = jnp.mean(gdy * xh, axis=-1, keepdims=True)
            return inv * (gdy - a - xh * c)

        def high_keys(b, hp):
            ds = back_half(l, b, hp, 1, True)
            e_s[l, b, hp * 2, :, SH:] = ds[:, :SH]
            e_s[l, b, hp * 2 + 1, :, SH:] = ds[:, SH:]

        def low_keys(b, hp):
            ds = back_half(l, b, hp, 0, False)
            back_queries(
                l, b, hp, ds, (e_s[l, b, hp * 2, :, SH:], e_s[l, b, hp * 2 + 1, :, SH:])
            )

        def prompt_gradient():
            base = TK // 16 * 16
            lhs = jnp.concatenate(
                [wide[b * S + base : (b + 1) * S, D : 3 * D] for b in range(B)], axis=0
            )
            full = mm_nt(lhs, w_qkv[l, :, D : 3 * D])
            n = S - base
            dprom = full[TK - base : n]
            for b in range(1, B):
                dprom = dprom + full[b * n + TK - base : (b + 1) * n]
            xh_p = xh1[l, base:S, :].astype(F32)[TK - base :]
            return ln_back(dprom, xh_p, r1[l, TK:S, :])

        pairs_loop(high_keys, 0, pairs)
        if above < L:
            reduce_ranks(above)
        reduce_start(l, prompt_gradient())
        if last:
            pairs_loop(low_keys, 0, pairs // 4)
            reduce_pair(l)
            pairs_loop(low_keys, pairs // 4, pairs * 3 // 4)
            reduce_group(l)
            pairs_loop(low_keys, pairs * 3 // 4, pairs)
        else:
            pairs_loop(low_keys, 0, pairs)
        if above < L:
            reduce_end(above)
        lhs = jnp.concatenate([wide[b * S : b * S + TQ, :] for b in range(B)], axis=0)
        acc[...] = mm_nt(lhs, w_qkv[l])
        if last:
            reduce_ranks(l)
        for b in range(B):

            def ln_one_back(row, b=b):
                at = pl.ds(pl.multiple_of(b * TQ + row, 16), 16)
                dx = ln_back(
                    acc[at, :],
                    xh1[l, pl.ds(pl.multiple_of(b * S + row, 16), 16), :].astype(F32),
                    r1[l, pl.ds(pl.multiple_of(b * S + row, 16), 16), :],
                )
                hid[at, :] = hid[at, :] + dx

            rows_loop(TK // 16 * 16, 16, ln_one_back, unroll=2)
            base = TK // 16 * 16
            if base < TK:
                dx = ln_back(
                    acc[b * TQ + base : b * TQ + TK, :],
                    xh1[l, b * S + base : b * S + base + 16, :].astype(F32)[: TK - base],
                    r1[l, b * S + base : b * S + TK, :],
                )
                hid[b * TQ + base : b * TQ + TK, :] = hid[b * TQ + base : b * TQ + TK, :] + dx

    for j in range(NJ):
        for b in range(B):
            stage_v[j, pl.ds(b, T, stride=B), :] = hid[
                b * TQ : b * TQ + T, 128 * j : 128 * (j + 1)
            ]
        leave(stage_nat.at[j], igrad_hbm.at[:, :, 128 * j : 128 * (j + 1)])
    reduce_end(0)

    grad_v = adam_nat.at[2].reshape(HJ, G * PB * L, 128)
    for l in range(L):
        for k in range(G):
            for j in range(HJ):
                grad_v[j, pl.ds(k * PB * L + l, PB, stride=L), :] = fin[l, k, j].astype(F32)
    n = PN * L
    squares = jnp.zeros((1, 1), F32)
    for j in range(HJ):
        rows = grad_v[j, 0:n, :]
        squares += jnp.sum(rows * rows, axis=(0, 1), keepdims=True)
    sq[core] = jnp.broadcast_to(squares, (8, 128))
    copy = pltpu.make_async_remote_copy(
        src_ref=sq.at[core],
        dst_ref=sq.at[core],
        send_sem=sem_sq.at[0],
        recv_sem=sem_sq.at[1],
        device_id={"mlp": other},
        device_id_type=MESH,
    )
    copy.start()
    for j in range(HJ):
        leave(adam_nat.at[2, j, 0:PN], pgrad_hbm.at[:, :, 128 * j : 128 * (j + 1)])
    copy.wait()
    grad_norm = jnp.sqrt(sq[0] + sq[1])
    norm_s[...] = grad_norm[0:1, 0:1]
    leave(norm_s, norm_hbm)
    factor = jnp.minimum(1.0, clip_limit / (grad_norm[0:1, :] + 1e-06))
    fix_first = 1.0 - beta_one**STEP
    fix_second = 1.0 - beta_two**STEP
    for j in range(HJ):
        local[f"first{j}"].wait()
        local[f"second{j}"].wait()
        first_v = adam_nat.at[0].reshape(HJ, G * PB * L, 128)
        second_v = adam_nat.at[1].reshape(HJ, G * PB * L, 128)
        clipped = grad_v[j, 0:n, :] * factor
        new_first = beta_one * first_v[j, 0:n, :] + (1.0 - beta_one) * clipped
        new_second = beta_two * second_v[j, 0:n, :] + (1.0 - beta_two) * clipped * clipped
        first_v[j, 0:n, :] = new_first
        second_v[j, 0:n, :] = new_second
        old = prom_v[core * HJ + j]
        prom_v[core * HJ + j] = old - learn_rate * (
            new_first / fix_first / (jnp.sqrt(new_second / fix_second) + adam_eps)
            + weight_decay * old
        )
        cols = slice(128 * j, 128 * (j + 1))
        leave(adam_nat.at[0, j, 0:PN], new_first_hbm.at[:, :, cols])
        leave(adam_nat.at[1, j, 0:PN], new_second_hbm.at[:, :, cols])
        leave(prom_nat.at[core * HJ + j], new_prompt_hbm.at[:, :, cols])
    for copy in leaving:
        copy.wait()


def hand_on_kernel(parts, *refs):
    n = len(parts)
    sources, targets, held, sem_in, sem_out = (
        refs[:n], refs[n : 2 * n], refs[2 * n : 3 * n], refs[3 * n], refs[3 * n + 1]
    )
    come, go = [], []
    for src, dst, mid, count in zip(sources, targets, held, parts):
        rows = src.shape[0]
        for i in range(count):
            lo, hi = rows * i // count, rows * (i + 1) // count
            a, b, c = (src, mid, dst) if count == 1 else (r.at[lo:hi] for r in (src, mid, dst))
            come.append(pltpu.make_async_copy(a, b, sem_in.at[len(come)]))
            go.append(pltpu.make_async_copy(b, c, sem_out.at[len(go)]))
    for copy in come:
        copy.start()
    for first, second in zip(come, go):
        first.wait()
        second.start()
    for copy in go:
        copy.wait()


def hand_on(parts, arrays):
    any_spec = pl.BlockSpec(memory_space=pl.ANY)
    return pl.pallas_call(
        functools.partial(hand_on_kernel, parts),
        out_shape=tuple(jax.ShapeDtypeStruct(a.shape, a.dtype) for a in arrays),
        in_specs=[any_spec] * len(arrays),
        out_specs=(any_spec,) * len(arrays),
        scratch_shapes=[VMEM(a.shape, a.dtype) for a in arrays]
        + [DMA((sum(parts),)), DMA((sum(parts),))],
        compiler_params=pltpu.CompilerParams(vmem_limit_bytes=60 * 2**20),
    )(*arrays)


def native(x):
    return x.transpose(1, 0, 2)


def local(
    ndp, tokens, cotangent, prompts, first_moment, second_moment, norm_params, bias_rows,
    qkv_weight, out_weight, up_weight, up_bias, down_weight,
):
    B, T, D = tokens.shape
    L, PN, _ = prompts.shape
    FH = down_weight.shape[1]
    TK = up_to(T, 8)
    S = up_to(TK + up_to(PN, 8), 128)
    TQ = up_to(T, 16)
    G = 4
    R = ndp // G
    NJ, HJ, PB = D // 128, D // 256, 16
    dims = (B, T, D, L, PN, TK, S, TQ, FH, G, R)
    H = HEADS
    n_local = 2 * NJ + 3 * HJ + 3 + 4 * L
    n_remote = HJ + 1 + 2 * L
    n_out = 2 * NJ + 4 * HJ + 1
    scratch = [
        VMEM((NJ, T, B, 128), BF16),
        VMEM((NJ, T, B, 128), BF16),
        VMEM((NJ, T, B, 128), F32),
        VMEM((NJ, PN, L, 128), F32),
        VMEM((3, HJ, G * PB, L, 128), F32),
        VMEM((L, 4, D), F32),
        VMEM((L, 4, D), F32),
        VMEM((L, D, 3 * D), BF16),
        VMEM((L, D, D), BF16),
        VMEM((L, 2, D, FH), BF16),
        VMEM((2, L, FH), F32),
        VMEM((L, 2, FH, D), BF16),
        VMEM((B, S, D), F32),
        VMEM((B * TQ, D), F32),
        VMEM((B * TQ, D), F32),
        VMEM((B * S, 3 * D), BF16),
        VMEM((B * TQ, D), BF16),
        VMEM((L, B * S, D), BF16),
        VMEM((L, B * S, 1), F32),
        VMEM((L, B * TQ, D), BF16),
        VMEM((L, B * TQ, 1), F32),
        VMEM((L, B * TQ, D), BF16),
        VMEM((L, B * S, D), BF16),
        VMEM((L, B * S, D), BF16),
        VMEM((L, B, H, TQ, S), BF16),
        VMEM((L, B, TQ, D), F32),
        VMEM((L, B * TQ, D), BF16),
        VMEM((L, B * TQ, 2 * FH), BF16),
        VMEM((L, 2, G, HJ, PB, 128), F32),
        VMEM((L, 2, G, HJ, PB, 128), BF16),
        VMEM((L, G, HJ, PB, 128), BF16),
        VMEM((L, G, HJ, PB, 128), F32),
        VMEM((L, G, HJ, PB, 128), BF16),
        VMEM((L, G, HJ, PB, 128), BF16),
        VMEM((L, R, HJ, PB, 128), BF16),
        VMEM((L, G, HJ, PB, 128), BF16),
        VMEM((2, 8, 128), F32),
        VMEM((1, 1), F32),
        DMA((n_local,)),
        DMA((n_out,)),
        DMA((n_remote,)),
        DMA((n_remote,)),
        DMA((L, 2)),
        DMA((L, G)),
        DMA((L, G)),
        DMA((L, R)),
        DMA((L, R)),
        DMA((L, G)),
        DMA((L, G)),
        DMA((2,)),
    ]
    any_spec = pl.BlockSpec(memory_space=pl.ANY)
    small = jax.ShapeDtypeStruct((PN, L, D // 2), F32)
    results = pl.pallas_call(
        functools.partial(main_kernel, dims),
        out_shape=(
            jax.ShapeDtypeStruct((T, B, D), BF16),
            jax.ShapeDtypeStruct((T, B, D), F32),
            small,
            jax.ShapeDtypeStruct((1, 1), F32),
            small,
            small,
            small,
        ),
        in_specs=[any_spec] * 12,
        out_specs=(any_spec,) * 7,
        scratch_shapes=scratch,
        compiler_params=pltpu.CompilerParams(
            collective_id=0, has_side_effects=True, vmem_limit_bytes=64 * 2**20
        ),
    )(
        native(tokens), native(cotangent), native(prompts), native(first_moment),
        native(second_moment), norm_params, bias_rows, qkv_weight, out_weight,
        up_weight, up_bias, down_weight,
    )
    act, igrad, grad, norm, new_first, new_second, new_prompts = hand_on(
        (4, 8, 1, 1, 1, 1, 1), results
    )
    return (
        native(act), native(igrad), native(grad), norm.reshape(()),
        native(new_first), native(new_second), native(new_prompts),
    )


def solution(mesh):
    ndp = mesh.shape["dp"]
    return jax.shard_map(
        functools.partial(local, ndp),
        mesh=mesh,
        in_specs=(
            P(("dp", "mlp"), None, None),
            P(("dp", "mlp"), None, None),
            P(None, None, "mlp"),
            P(None, None, "mlp"),
            P(None, None, "mlp"),
            P(),
            P(),
            P(),
            P(),
            P(None, None, "mlp"),
            P(None, "mlp"),
            P(None, "mlp", None),
        ),
        out_specs=(
            P(("dp", "mlp"), None, None),
            P(("dp", "mlp"), None, None),
            P(None, None, "mlp"),
            P(),
            P(None, None, "mlp"),
            P(None, None, "mlp"),
            P(None, None, "mlp"),
        ),
        check_vma=False,
    )
```

time: 130 us -> 92.1 us (0.71)
  local copies, waits for them, and re-layouts: 20.6 us -> 0 us
  Pallas kernels: 107 us -> 91.2 us
  between operations: 2.35 us -> 0.83 us
    unnamed x11 -> x0, local copies, waits for them, and re-layouts: 20.6 us -> none
    pallas_call x2, Pallas kernels: 107 us -> 91.2 us  [the longest x1 87.7 us: local(): pl.pallas_call(functools.partial(main_kernel, dims), out_shape=(jax.Shape...]
where the time goes in v1:
time: 92.1 us; the launch traced here: 92 us
  Pallas kernels  91.2 us (99%)
    pallas_call x1, Pallas kernels, local(): pl.pallas_call(functools.partial(main_kernel, dims), out_shape=(jax.Shape...  87.7 us
    pallas_call x1, Pallas kernels, hand_on(): pl.pallas_call(functools.partial(hand_on_kernel, parts), out_shape=tuple(...  3.41 us

profile of v1, /device:TPU:0, one launch (start us, length us, event | category | flops | bytes accessed | tf_op | source)
XLA Modules:
  0.0 92.0 jit_solution(16434837576500723132)
XLA Ops:
  0.6 87.7 %shard_map.171 = (bf16[197,2,768]{2,1,0:T(2,128)(2,1)}, f32[197,2,768]{2,1,0:T(2,128)}, f32[50,2,384]{2,1,0:T(2,128)}, f32[1,1]{1,0:T(1,128)}, f32[50,2,384]{2,1...) custom-call(bf16[197,2,768]{2,1,0:T(2,128)(2,1)} %bitcast.12, bf16[197,2,768]{2,1,0:T(2,128)(2,1)} %bitcast.13, ...), custom_call_target="tpu_custom_call" | custom-call | tf_op jit(solution)/shard_map/pallas_call | solution.py:815
  88.4 3.4 %shard_map.172 = (bf16[197,2,768]{2,1,0:T(2,128)(2,1)}, f32[197,2,768]{2,1,0:T(2,128)}, f32[50,2,384]{2,1,0:T(2,128)}, f32[1,1]{1,0:T(1,128)}, f32[50,2,384]{2,1...) custom-call(bf16[197,2,768]{2,1,0:T(2,128)(2,1)} %get-tuple-element.21.refs_0_, ...), custom_call_target="tpu_custom_call" | custom-call | tf_op jit(solution)/shard_map/pallas_call | solution.py:728
